TPU v7x, 32 devices: a whole 2x2x4 slice. The times are simulated.
32 devices in a mesh: groups: 2 (over y), expert: 8 (over z, x), tensor: 2 (over core).
Axes of the slice: x: 2, y: 2, z: 4, core: 2. Of those that a mesh axis runs over, the one named last changes fastest.
Arguments:
- tokens: bfloat16 [2, 1024, 2048], P(None, ('groups', 'expert')), parts along dimension 1, may hold values from -6 to 6
- routes: int32 [2, 1024, 8], P(None, ('groups', 'expert')), parts along dimension 1, may hold values from 0 to 7, as said below
- probs: float32 [2, 1024, 8], P(None, ('groups', 'expert')), parts along dimension 1, may hold values from 0.02 to 0.3
- up_weight: bfloat16 [8, 2048, 768], P('expert', None, 'tensor'), may hold values from -0.125 to 0.125
- down_weight: bfloat16 [8, 768, 2048], P('expert', None, 'tensor'), may hold values from -0.21875 to 0.21875
- old_place: int32 [16], P('groups'), parts along dimension 0, may hold values from 0 to 7, as said below
- new_place: int32 [32], P('groups'), parts along dimension 0, may hold values from 0 to 7, as said below
Outputs:
- mixed: bfloat16 [2, 1024, 2048], P(None, ('groups', 'expert'), 'tensor'), parts along dimension 1
- slot_rows: int32 [32], P(('groups', 'expert')), parts along dimension 0
There are 2 independent parts, one for each index of `groups`. A program takes and returns all parts, laid end to end along the dimension named above; an argument that names none is the same for every part. Nothing has to cross between parts.
Inputs may be any that keep to these rules, and one draw needn't show every extreme that they name: `routes`: each token names 8 different experts. `old_place`: each expert is held by exactly one old slot. `new_place`: new slot 2 * s holds the expert of old slot s; no expert is held by more than 4 new slots, and some expert by exactly 4.
All inputs are finite; a program needn't handle non-finite values.
Results may differ from a plain program's by a relative error of at most 0.0058.
Values may be sent and summed in bfloat16 or wider, within the bound.
A program may use at most 128 MiB of HBM per device.

v0:
```python
import jax
import jax.numpy as jnp
from jax import lax
from jax.sharding import PartitionSpec as P

REPLICAS = 4


def earlier_same(labels):
    positions = jnp.arange(labels.shape[0], dtype=jnp.int32)
    earlier = positions[None, :] < positions[:, None]
    same_label = labels[:, None] == labels[None, :]
    return jnp.sum((earlier & same_label).astype(jnp.int32), axis=1)


def holder_index(labels, holders):
    matches = labels[:, None] == holders[None, :]
    positions = jnp.arange(holders.shape[0], dtype=jnp.int32)
    return jnp.sum(matches.astype(jnp.int32) * positions[None, :], axis=1)


def replica_slots(flat_routes, new_place, source_index):
    positions = jnp.arange(new_place.shape[0], dtype=jnp.int32)
    same_slot = new_place[:, None] == new_place[None, :]
    occurrence = jnp.sum(
        (same_slot & (positions[None, :] < positions[:, None])).astype(jnp.int32), axis=1
    )
    matches = flat_routes[:, None] == new_place[None, :]
    replicas = jnp.sum(matches.astype(jnp.int32), axis=1)
    wanted = (earlier_same(flat_routes) + source_index) % replicas
    chosen = matches & (occurrence[None, :] == wanted[:, None])
    slot_ids = jnp.sum(chosen.astype(jnp.int32) * positions[None, :], axis=1)
    return (slot_ids, chosen)


def capacity_for(block_rows, targets, token_count):
    return min(token_count, max(2, (5 * block_rows + 4 * targets - 1) // (4 * targets)))


def serve_cells(tokens_mb, probs_mb, cell_ids, target_count, block, up_local, down_local):
    token_count = tokens_mb.shape[0]
    topk_count = cell_ids.shape[0] // token_count
    slots_here = up_local.shape[0]
    cells = jnp.arange(target_count * block, dtype=jnp.int32)
    placed = (cells[:, None] == cell_ids[None, :]).astype(jnp.bfloat16)
    by_token = jnp.sum(placed.reshape(target_count * block, token_count, topk_count), axis=2)
    send_rows = jnp.dot(by_token, tokens_mb, preferred_element_type=jnp.float32).astype(
        jnp.bfloat16
    )
    send_rows = send_rows.reshape(target_count, block, -1)
    received = lax.all_to_all(send_rows, "expert", split_axis=0, concat_axis=0, tiled=True)
    sources = received.shape[0] // slots_here
    grid = received.reshape(sources, slots_here, received.shape[1], received.shape[2])
    hidden = jax.nn.silu(
        jnp.einsum("nscd,sdf->nscf", grid, up_local, preferred_element_type=jnp.float32)
    ).astype(jnp.bfloat16)
    hidden = lax.all_gather(hidden, "tensor", axis=3, tiled=True)
    outputs = jnp.einsum(
        "nscf,sfd->nscd", hidden, down_local, preferred_element_type=jnp.float32
    ).astype(jnp.bfloat16)
    outputs = outputs.reshape(received.shape[0], received.shape[1], -1)
    returned = lax.all_to_all(outputs, "expert", split_axis=0, concat_axis=0, tiled=True)
    flat_back = returned.reshape(target_count * block, -1)
    picked = lax.dot_general(
        placed, flat_back, (((0,), (0,)), ((), ())), preferred_element_type=jnp.float32
    )
    weighted = picked.reshape(token_count, topk_count, -1) * probs_mb[:, :, None]
    return jnp.sum(weighted, axis=1).astype(jnp.bfloat16)


def on_device(tokens, routes, probs, up_weight, down_weight, old_place, new_place):
    source_index = lax.axis_index("expert")
    devices = lax.axis_size("expert")
    token_count = tokens.shape[1]
    topk_count = routes.shape[2]
    block_rows = token_count * topk_count
    expert_count = old_place.shape[0]
    slot_count = new_place.shape[0]
    early_cap = capacity_for(block_rows, expert_count, token_count)
    later_cap = capacity_for(block_rows, slot_count, token_count)
    early_routes = routes[0].reshape(-1)
    later_routes = routes[1].reshape(-1)
    early_slots = holder_index(early_routes, old_place)
    early_rank = earlier_same(early_slots)
    early_cells = jnp.where(early_rank < early_cap, early_slots * early_cap + early_rank, -1)
    later_slots, chosen = replica_slots(later_routes, new_place, source_index)
    slot_counts = lax.psum(jnp.sum(chosen.astype(jnp.int32), axis=0), "expert")
    slot_dev = slot_count // devices
    slot_rows = lax.dynamic_slice_in_dim(slot_counts, source_index * slot_dev, slot_dev, 0)
    later_rank = earlier_same(later_slots)
    later_kept = later_rank < later_cap
    early_out = serve_cells(
        tokens[0], probs[0], early_cells, expert_count, early_cap, up_weight, down_weight
    )
    homes = holder_index(later_routes, old_place)
    home_block = min(token_count, REPLICAS * later_cap)
    home_labels = jnp.where(later_kept, homes, -1)
    home_rank = earlier_same(home_labels)
    later_cells = jnp.where(later_kept, homes * home_block + home_rank, -1)
    later_out = serve_cells(
        tokens[1], probs[1], later_cells, expert_count, home_block, up_weight, down_weight
    )
    return (jnp.stack([early_out, later_out]), slot_rows)


def solution(mesh):
    placed = (
        P(None, ("groups", "expert"), None),
        P(None, ("groups", "expert"), None),
        P(None, ("groups", "expert"), None),
        P("expert", None, "tensor"),
        P("expert", None, "tensor"),
        P("groups"),
        P("groups"),
    )
    return jax.shard_map(
        on_device,
        mesh=mesh,
        in_specs=placed,
        out_specs=(P(None, ("groups", "expert"), "tensor"), P(("groups", "expert"))),
        check_vma=False,
    )
```

profile of v0, /device:TPU:0, one launch (start us, length us, event | category | flops | bytes accessed | tf_op | source)
XLA Modules:
  0.0 182.2 jit_solution(15727923861722691015)
XLA Ops:
  0.6 0.8 fusion.46
  1.9 0.7 fusion.44
  2.7 0.9 convert_reduce_fusion.5
  3.7 0.9 convert_reduce_fusion.4
  5.0 0.7 select_reduce_fusion.2
  6.7 3.0 %convolution_convert_fusion.1 = bf16[512,2048]{1,0:T(8,128)(2,1)} fusion(bf16[512,64]{0,1:T(8,128)(2,1)S(1)} %fusion.37, bf16[2,64,2048]{2,1,0:T(8,128)(2,1)} %param.7), kind=kOutput, calls=%fused_computation.1 | convolution fusion | flops 135266304 | bytes 2424832 | tf_op jit(solution)/shard_map/dot_general | solution.py:47
  9.8 7.4 %all-to-all-start = ((bf16[8,64,2048]{2,1,0:T(8,128)(2,1)}), bf16[8,64,2048]{2,1,0:T(8,128)(2,1)}, u32[]{:S(2)}, u32[]{:S(2)}) async-start(bf16[8,64,2048]{2,1,0:T(8,128)(2,1)} %bitcast.83), calls=%async_computation | async-start | bytes 4194304 | tf_op jit(solution)/shard_map/all_to_all | solution.py:51
  17.6 2.1 %convolution_convert_fusion = bf16[512,2048]{1,0:T(8,128)(2,1)} fusion(bf16[512,64]{0,1:T(8,128)(2,1)S(1)} %fusion.36, bf16[2,64,2048]{2,1,0:T(8,128)(2,1)S(1)} %copy-done.1), kind=kOutput, calls=%fused_computation | convolution fusion | flops 135266304 | bytes 2424832 | tf_op jit(solution)/shard_map/dot_general | solution.py:47
  19.7 45.8 %all-to-all-done = bf16[8,64,2048]{2,1,0:T(8,128)(2,1)} async-done(((bf16[8,64,2048]{2,1,0:T(8,128)(2,1)}), bf16[8,64,2048]{2,1,0:T(8,128)(2,1)}, u32[]{:S(2)}, u32[]{:S(2)}) %all-to-all-start) | async-done | bytes 2097184 | tf_op jit(solution)/shard_map/all_to_all | solution.py:51
  65.5 4.3 %all-to-all-start.2 = ((bf16[8,64,2048]{2,1,0:T(8,128)(2,1)}), bf16[8,64,2048]{2,1,0:T(8,128)(2,1)}, u32[]{:S(2)}, u32[]{:S(2)}) async-start(bf16[8,64,2048]{2,1,0:T(8,128)(2,1)} %bitcast.82), calls=%async_computation.2 | async-start | bytes 4194304 | tf_op jit(solution)/shard_map/all_to_all | solution.py:51
  69.8 3.4 %multiply_convert_fusion.1 = bf16[8,1,64,384]{3,2,0,1:T(8,128)(2,1)S(1)} fusion(bf16[8,64,2048]{2,1,0:T(8,128)(2,1)} %all-to-all-done, bf16[1,2048,384]{2,1,0:T(8,128)(2,1)} %param.10), kind=kOutput, calls=%fused_computation.36 | convolution fusion | flops 806289408 | bytes 4063232 | tf_op jit(solution)/shard_map/nscd,sdf->nscf/dot_general | solution.py:55
  73.2 2.4 %all_gather.6 = bf16[8,1,64,768]{3,2,0,1:T(8,128)(2,1)S(1)} all-gather(bf16[8,1,64,384]{3,2,0,1:T(8,128)(2,1)S(1)} %multiply_convert_fusion.1), channel_id=1, replica_groups=mesh['groups'=2,'expert'=8,'tensor'=2] {'tensor'}, dimensions={3}, use_global_device_ids=true | all-gather | bytes 1179648 | tf_op jit(solution)/shard_map/all_gather | solution.py:57
  75.6 2.0 %fusion.8 = bf16[8,64,1024]{2,1,0:T(8,128)(2,1)} fusion(bf16[1,768,1024]{2,1,0:T(8,128)(2,1)S(1)} %copy-done, bf16[8,1,64,768]{3,2,0,1:T(8,128)(2,1)S(1)} %all_gather.6), kind=kOutput, calls=%fused_computation.12 | convolution fusion | flops 805830656 | bytes 3407872 | tf_op jit(solution)/shard_map/nscf,sfd->nscd/dot_general | solution.py:58
  77.5 40.1 %all-to-all-done.2 = bf16[8,64,2048]{2,1,0:T(8,128)(2,1)} async-done(((bf16[8,64,2048]{2,1,0:T(8,128)(2,1)}), bf16[8,64,2048]{2,1,0:T(8,128)(2,1)}, u32[]{:S(2)}, u32[]{:S(2)}) %all-to-all-start.2) | async-done | bytes 2097184 | tf_op jit(solution)/shard_map/all_to_all | solution.py:51
  117.7 3.6 %all-to-all-start.1 = ((bf16[8,64,1024]{2,1,0:T(8,128)(2,1)}), bf16[8,64,1024]{2,1,0:T(8,128)(2,1)S(1)}, u32[]{:S(2)}, u32[]{:S(2)}) async-start(bf16[8,64,1024]{2,1,0:T(8,128)(2,1)} %fusion.8), calls=%async_computation.1 | async-start | bytes 2097152 | tf_op jit(solution)/shard_map/all_to_all | solution.py:62
  121.3 3.4 %multiply_convert_fusion = bf16[8,1,64,384]{3,2,0,1:T(8,128)(2,1)S(1)} fusion(bf16[8,64,2048]{2,1,0:T(8,128)(2,1)} %all-to-all-done.2, bf16[1,2048,384]{2,1,0:T(8,128)(2,1)} %param.10), kind=kOutput, calls=%fused_computation.35 | convolution fusion | flops 806289408 | bytes 4063232 | tf_op jit(solution)/shard_map/nscd,sdf->nscf/dot_general | solution.py:55
  124.7 2.4 %all_gather.7 = bf16[8,1,64,768]{3,2,0,1:T(8,128)(2,1)S(1)} all-gather(bf16[8,1,64,384]{3,2,0,1:T(8,128)(2,1)S(1)} %multiply_convert_fusion), channel_id=1, replica_groups=mesh['groups'=2,'expert'=8,'tensor'=2] {'tensor'}, dimensions={3}, use_global_device_ids=true | all-gather | bytes 1179648 | tf_op jit(solution)/shard_map/all_gather | solution.py:57
  127.0 2.0 %fusion.11 = bf16[8,64,1024]{2,1,0:T(8,128)(2,1)} fusion(bf16[1,768,1024]{2,1,0:T(8,128)(2,1)S(1)} %copy-done, bf16[8,1,64,768]{3,2,0,1:T(8,128)(2,1)S(1)} %all_gather.7), kind=kOutput, calls=%fused_computation.13 | convolution fusion | flops 805830656 | bytes 3407872 | tf_op jit(solution)/shard_map/nscf,sfd->nscd/dot_general | solution.py:58
  129.0 18.2 %all-to-all-done.1 = bf16[8,64,1024]{2,1,0:T(8,128)(2,1)S(1)} async-done(((bf16[8,64,1024]{2,1,0:T(8,128)(2,1)}), bf16[8,64,1024]{2,1,0:T(8,128)(2,1)S(1)}, u32[]{:S(2)}, u32[]{:S(2)}) %all-to-all-start.1) | async-done | bytes 1048608 | tf_op jit(solution)/shard_map/all_to_all | solution.py:62
  147.2 4.2 %all-to-all-start.3 = ((bf16[8,64,1024]{2,1,0:T(8,128)(2,1)}), bf16[8,64,1024]{2,1,0:T(8,128)(2,1)}, u32[]{:S(2)}, u32[]{:S(2)}) async-start(bf16[8,64,1024]{2,1,0:T(8,128)(2,1)} %fusion.11), calls=%async_computation.3 | async-start | bytes 2097152 | tf_op jit(solution)/shard_map/all_to_all | solution.py:62
  151.5 25.8 %psum.7 = s32[16]{0:T(128)S(1)} all-reduce(s32[16]{0:T(128)S(1)} %get-tuple-element.2), channel_id=1, replica_groups=mesh['groups'=2,'expert'=8,'tensor'=2] {'expert'}, use_global_device_ids=true, to_apply=%region_14.15 | all-reduce | flops 16 | bytes 128 | tf_op jit(solution)/shard_map/psum | solution.py:87
  178.0 1.1 multiply_reduce_fusion.1
  179.1 2.3 %multiply_reduce_fusion = bf16[64,1024]{1,0:T(8,128)(2,1)S(1)} fusion(bf16[512,1024,1]{1,0,2:T(8,128)(2,1)} %bitcast.27, f32[64,8]{1,0:T(8,128)S(1)} %copy.18, s32[512]{0:T(512)S(1)} %get-tuple-element.12), kind=kOutput, calls=%fused_computation.2 | convolution fusion | flops 538116096 | bytes 1183744 | tf_op jit(solution)/shard_map/dot_general | solution.py:64
  181.5 0.7 pad_maximum_fusion
  (26 shorter events, 3.2 us)
Async XLA Ops:
  0.6 74.9 %copy-start = (bf16[1,768,1024]{2,1,0:T(8,128)(2,1)S(1)}, bf16[1,768,1024]{2,1,0:T(8,128)(2,1)}, u32[]{:S(2)}) copy-start(bf16[1,768,1024]{2,1,0:T(8,128)(2,1)} %param.11) | copy-start | bytes 4718596
  9.8 7.9 %copy-start.1 = (bf16[2,64,2048]{2,1,0:T(8,128)(2,1)S(1)}, bf16[2,64,2048]{2,1,0:T(8,128)(2,1)}, u32[]{:S(2)}) copy-start(bf16[2,64,2048]{2,1,0:T(8,128)(2,1)} %param.7) | copy-start | bytes 1572868
  9.8 55.7 %all-to-all-start = ((bf16[8,64,2048]{2,1,0:T(8,128)(2,1)}), bf16[8,64,2048]{2,1,0:T(8,128)(2,1)}, u32[]{:S(2)}, u32[]{:S(2)}) async-start(bf16[8,64,2048]{2,1,0:T(8,128)(2,1)} %bitcast.83), calls=%async_computation | async-start | bytes 4194304 | tf_op jit(solution)/shard_map/all_to_all | solution.py:51
  65.5 52.2 %all-to-all-start.2 = ((bf16[8,64,2048]{2,1,0:T(8,128)(2,1)}), bf16[8,64,2048]{2,1,0:T(8,128)(2,1)}, u32[]{:S(2)}, u32[]{:S(2)}) async-start(bf16[8,64,2048]{2,1,0:T(8,128)(2,1)} %bitcast.82), calls=%async_computation.2 | async-start | bytes 4194304 | tf_op jit(solution)/shard_map/all_to_all | solution.py:51
  117.7 29.6 %all-to-all-start.1 = ((bf16[8,64,1024]{2,1,0:T(8,128)(2,1)}), bf16[8,64,1024]{2,1,0:T(8,128)(2,1)S(1)}, u32[]{:S(2)}, u32[]{:S(2)}) async-start(bf16[8,64,1024]{2,1,0:T(8,128)(2,1)} %fusion.8), calls=%async_computation.1 | async-start | bytes 2097152 | tf_op jit(solution)/shard_map/all_to_all | solution.py:62
  129.0 48.2 %copy-start.2 = (f32[2,64,8]{1,2,0:T(8,128)S(1)}, f32[2,64,8]{1,2,0:T(8,128)}, u32[]{:S(2)}) copy-start(f32[2,64,8]{1,2,0:T(8,128)} %param.9) | copy-start | bytes 12292
  147.2 31.9 %all-to-all-start.3 = ((bf16[8,64,1024]{2,1,0:T(8,128)(2,1)}), bf16[8,64,1024]{2,1,0:T(8,128)(2,1)}, u32[]{:S(2)}, u32[]{:S(2)}) async-start(bf16[8,64,1024]{2,1,0:T(8,128)(2,1)} %fusion.11), calls=%async_computation.3 | async-start | bytes 2097152 | tf_op jit(solution)/shard_map/all_to_all | solution.py:62
where the time goes:
time: 183 us; the launch traced here: 182 us
  waiting for transfers between devices  104 us (57%)
  blocking collectives  30.5 us (17%)
  starting transfers between devices  19.6 us (11%)
  matrix products  19.2 us (10%)
  other arithmetic  5.9 us (3%)
  local copies, waits for them, and re-layouts  2.12 us (1%)
    all_to_all x2, waiting for transfers between devices, serve_cells(): lax.all_to_all(send_rows, 'expert', split_axis=0, concat_axis=0, tiled=True)  85.9 us
    psum x1, blocking collectives, on_device(): slot_counts = lax.psum(jnp.sum(chosen.astype(jnp.int32), axis=0), 'expert')  25.8 us
    all_to_all x2, waiting for transfers between devices, serve_cells(): lax.all_to_all(outputs, 'expert', split_axis=0, concat_axis=0, tiled=True)  18.2 us
    all_to_all x2, starting transfers between devices, serve_cells(): lax.all_to_all(send_rows, 'expert', split_axis=0, concat_axis=0, tiled=True)  11.7 us
    all_to_all x2, starting transfers between devices, serve_cells(): lax.all_to_all(outputs, 'expert', split_axis=0, concat_axis=0, tiled=True)  7.86 us
    dot_general x2, matrix products, serve_cells(): jnp.einsum('nscd,sdf->nscf', grid, up_local, preferred_element_type=jnp.f...  6.73 us
    dot_general x2, matrix products, serve_cells(): jnp.dot(by_token, tokens_mb, preferred_element_type=jnp.float32)  5.09 us
    all_gather x2, blocking collectives, serve_cells(): hidden = lax.all_gather(hidden, 'tensor', axis=3, tiled=True)  4.74 us
  transfers between devices with their start and end apart: 4, of which 3 were waited for; matrix products, arithmetic and copies ran while one was open for 8% of the time, Pallas kernels for 0%

commit v1 on v0

--- a/solution.py
+++ b/solution.py
@@ -1,7 +1,13 @@
+import functools
+
 import jax
 import jax.numpy as jnp
 from jax import lax
+from jax.experimental import pallas as pl
+from jax.experimental.pallas import tpu as pltpu
 from jax.sharding import PartitionSpec as P
+
+MESH = pl.DeviceIdType.MESH
 
 REPLICAS = 4
 
@@ -103,6 +109,249 @@
     return (jnp.stack([early_out, later_out]), slot_rows)
 
 
+def dense_weights(routes, probs, old_place, new_place):
+    token_count = routes.shape[1]
+    block_rows = token_count * routes.shape[2]
+    early_cap = capacity_for(block_rows, old_place.shape[0], token_count)
+    later_cap = capacity_for(block_rows, new_place.shape[0], token_count)
+    replicas = jnp.sum((old_place[:, None] == new_place[None, :]).astype(jnp.int32), axis=1)
+    rank = jnp.arange(token_count, dtype=jnp.int32)[None, :]
+    early_kept = jnp.broadcast_to(rank < early_cap, (old_place.shape[0], token_count))
+    later_kept = rank < later_cap * replicas[:, None]
+    kept = jnp.stack([early_kept, later_kept])
+    same = routes[:, None, :, :] == old_place[None, :, None, None]
+    weights = jnp.sum(jnp.where(same, probs[:, None, :, :], 0.0), axis=3)
+    return jnp.where(kept, weights, 0.0)
+
+
+def dense_slot_rows(new_place, source_index, devices, token_count):
+    slot_count = new_place.shape[0]
+    slot_dev = slot_count // devices
+    positions = jnp.arange(slot_count, dtype=jnp.int32)
+    same = new_place[:, None] == new_place[None, :]
+    replicas = jnp.sum(same.astype(jnp.int32), axis=1)
+    earlier = positions[None, :] < positions[:, None]
+    occurrence = jnp.sum((same & earlier).astype(jnp.int32), axis=1)
+    places = jnp.arange(token_count, dtype=jnp.int32)[:, None] + jnp.arange(devices, dtype=jnp.int32)[None, :]
+    hits = (places[None] % replicas[:, None, None]) == occurrence[:, None, None]
+    counts = jnp.sum(hits.astype(jnp.int32), axis=(1, 2))
+    return lax.dynamic_slice_in_dim(counts, source_index * slot_dev, slot_dev, 0)
+
+
+def expert_kernel(
+    n, chunks, tok, wts, up, down, out,
+    xall, wall, upv, downv, acc, psend, xrecv, zsend, zrecv, res,
+    loc, tw_s, tw_r, w_s, w_r, az_s, az_r, ax_s, ax_r, rx_s, rx_r, rz_s, rz_r,
+):
+    e = lax.axis_index("expert")
+    core = lax.axis_index("tensor")
+    column = n // 2
+    x = lax.rem(e, 2)
+    z = e // 2
+    pair = e + 1 - 2 * x
+    rows, width = xall.shape[1], xall.shape[2]
+    step_rows = rows // chunks
+    up_half = up.shape[2]
+    halves = downv.shape[0]
+    half = downv.shape[2]
+
+    def remote(src, dst, send, recv, expert=None):
+        device = {"expert": expert} if expert is not None else {"tensor": 1 - core}
+        return pltpu.make_async_remote_copy(
+            src_ref=src, dst_ref=dst, send_sem=send, recv_sem=recv,
+            device_id=device, device_id_type=MESH,
+        )
+
+    def column_id(step):
+        return lax.rem(z - step + column, column)
+
+    def block(step, side):
+        return 2 * column_id(step) + side
+
+    local = [
+        pltpu.make_async_copy(tok.at[core], xall.at[e], loc.at[0]),
+        pltpu.make_async_copy(wts.at[core], wall.at[e], loc.at[1]),
+        pltpu.make_async_copy(
+            up.at[0], upv.at[:, pl.ds(pl.multiple_of(core * up_half, 128), up_half)], loc.at[2]
+        ),
+        pltpu.make_async_copy(down.at[0], downv.at[core], loc.at[3]),
+    ]
+    for copy in local:
+        copy.start()
+
+    barrier = pltpu.get_barrier_semaphore()
+    for shift in range(1, n):
+        pl.semaphore_signal(barrier, inc=1, device_id={"expert": lax.rem(e + shift, n)}, device_id_type=MESH)
+    pl.semaphore_signal(barrier, inc=1, device_id={"tensor": 1 - core}, device_id_type=MESH)
+    pl.semaphore_wait(barrier, n)
+
+    def part(k):
+        return pl.ds(k * step_rows, step_rows)
+
+    own_x, own_z, own_w = [], [], []
+    for k in range(chunks):
+        copy = remote(tok.at[core, part(k)], xall.at[e, part(k)], ax_s.at[0, k], ax_r.at[0, k], pair)
+        copy.start()
+        own_x.append(copy)
+    for s in range(1, column):
+        for k in range(chunks):
+            target = 2 * lax.rem(z + s, column) + x
+            copy = remote(tok.at[core, part(k)], xall.at[e, part(k)], az_s.at[s, k], az_r.at[s, k], target)
+            copy.start()
+            own_z.append(copy)
+    swap = [
+        remote(
+            up.at[0], upv.at[:, pl.ds(pl.multiple_of(core * up_half, 128), up_half)], tw_s.at[0], tw_r.at[0]
+        ),
+        remote(down.at[0], downv.at[core], tw_s.at[1], tw_r.at[1]),
+    ]
+    for copy in swap:
+        copy.start()
+    for s in range(1, n):
+        copy = remote(wts.at[core], wall.at[e], w_s.at[s], w_r.at[s], lax.rem(e + s, n))
+        copy.start()
+        own_w.append(copy)
+
+    sent = []
+
+    def relay(s):
+        b = block(s, x)
+        for k in range(chunks):
+            remote(tok.at[core, part(k)], xall.at[b, part(k)], az_s.at[s, k], az_r.at[s, k], pair).wait_recv()
+            copy = remote(xall.at[b, part(k)], xall.at[b, part(k)], ax_s.at[s, k], ax_r.at[s, k], pair)
+            copy.start()
+            sent.append(copy)
+
+    def arrived(s):
+        b = block(s, 1 - x)
+        for k in range(chunks):
+            remote(tok.at[core, part(k)], xall.at[b, part(k)], ax_s.at[s, k], ax_r.at[s, k], pair).wait_recv()
+
+    def scale_of(b):
+        row = wall[b, pl.ds(e, 1), :]
+        square = lax.broadcasted_iota(jnp.int32, (rows, rows), 0) == lax.broadcasted_iota(jnp.int32, (rows, rows), 1)
+        return jnp.sum(jnp.where(square, row, 0.0), axis=1, keepdims=True)
+
+    def hidden_of(b):
+        v = jnp.dot(xall[b], upv[...], preferred_element_type=jnp.float32)
+        return (v / (1.0 + jnp.exp(-v))).astype(jnp.bfloat16)
+
+    def keep(s):
+        b = block(s, x)
+        h = hidden_of(b)
+        scale = scale_of(b)
+        for q in range(halves):
+            acc[s, q] = jnp.dot(h, downv[q], preferred_element_type=jnp.float32) * scale
+
+    def give(s):
+        b = block(s, 1 - x)
+        h = hidden_of(b)
+        scale = scale_of(b)
+        for q in range(halves):
+            o = jnp.dot(h, downv[q], preferred_element_type=jnp.float32) * scale
+            psend[s, q] = o.astype(jnp.bfloat16)
+            copy = remote(psend.at[s, q], xrecv.at[s, q], rx_s.at[s, q], rx_r.at[s, q], pair)
+            copy.start()
+            sent.append(copy)
+
+    def pass_on(s):
+        for q in range(halves):
+            remote(psend.at[s, q], xrecv.at[s, q], rx_s.at[s, q], rx_r.at[s, q], pair).wait_recv()
+            zsend[s, q] = (acc[s, q] + xrecv[s, q].astype(jnp.float32)).astype(jnp.bfloat16)
+            copy = remote(zsend.at[s, q], zrecv.at[s, q], rz_s.at[s, q], rz_r.at[s, q], block(s, x))
+            copy.start()
+            sent.append(copy)
+
+    for copy in local:
+        copy.wait()
+    for copy in swap:
+        copy.wait_recv()
+    for s in range(1, n):
+        remote(wts.at[core], wall.at[lax.rem(e - s + n, n)], w_s.at[s], w_r.at[s], pair).wait_recv()
+    keep(0)
+    relay(1)
+    arrived(0)
+    give(0)
+    for s in range(1, column):
+        if s + 1 < column:
+            relay(s + 1)
+        keep(s)
+        arrived(s)
+        give(s)
+        if s > 1:
+            pass_on(s - 1)
+    if column > 1:
+        pass_on(column - 1)
+    for q in range(halves):
+        remote(psend.at[0, q], xrecv.at[0, q], rx_s.at[0, q], rx_r.at[0, q], pair).wait_recv()
+        total = acc[0, q] + xrecv[0, q].astype(jnp.float32)
+        for s in range(1, column):
+            remote(zsend.at[s, q], zrecv.at[s, q], rz_s.at[s, q], rz_r.at[s, q], pair).wait_recv()
+            total = total + zrecv[s, q].astype(jnp.float32)
+        res[q] = total.astype(jnp.bfloat16)
+    last = remote(res.at[1 - core], out.at[core], tw_s.at[2], tw_r.at[2])
+    last.start()
+    mine = pltpu.make_async_copy(res.at[core], out.at[core], loc.at[4])
+    mine.start()
+    for copy in own_x + own_z + own_w + swap + sent:
+        copy.wait_send()
+    mine.wait()
+    last.wait_send()
+    remote(res.at[1 - core], out.at[1 - core], tw_s.at[2], tw_r.at[2]).wait_recv()
+
+
+def dense_on_device(tokens, routes, probs, up_weight, down_weight, old_place, new_place):
+    source_index = lax.axis_index("expert")
+    n = lax.axis_size("expert")
+    batches, rows, width = tokens.shape
+    hidden_half, half = down_weight.shape[1] // 2, down_weight.shape[2]
+    column, chunks = n // 2, 2
+    slot_rows = dense_slot_rows(new_place, source_index, n, rows)
+    weights = dense_weights(routes, probs, old_place, new_place)
+    dma = pltpu.SemaphoreType.DMA
+    bf16, f32 = jnp.bfloat16, jnp.float32
+    mixed = pl.pallas_call(
+        functools.partial(expert_kernel, n, chunks),
+        out_shape=jax.ShapeDtypeStruct((batches, rows, half), bf16),
+        in_specs=[pl.BlockSpec(memory_space=pl.ANY)] * 4,
+        out_specs=pl.BlockSpec(memory_space=pl.ANY),
+        scratch_shapes=[
+            pltpu.VMEM((n, rows, width), bf16),
+            pltpu.VMEM((n, old_place.shape[0], rows), f32),
+            pltpu.VMEM((width, 2 * hidden_half), bf16),
+            pltpu.VMEM((2, 2 * hidden_half, half), bf16),
+            pltpu.VMEM((column, 2, rows, half), f32),
+            pltpu.VMEM((column, 2, rows, half), bf16),
+            pltpu.VMEM((column, 2, rows, half), bf16),
+            pltpu.VMEM((column, 2, rows, half), bf16),
+            pltpu.VMEM((column, 2, rows, half), bf16),
+            pltpu.VMEM((2, rows, half), bf16),
+            dma((5,)), dma((3,)), dma((3,)), dma((n,)), dma((n,)),
+            dma((column, chunks)), dma((column, chunks)), dma((column, chunks)), dma((column, chunks)),
+            dma((column, 2)), dma((column, 2)), dma((column, 2)), dma((column, 2)),
+        ],
+        compiler_params=pltpu.CompilerParams(
+            collective_id=0, has_side_effects=True, vmem_limit_bytes=40 * 1024 * 1024
+        ),
+    )(tokens, weights, up_weight, down_weight)
+    return (mixed, slot_rows)
+
+
+def choose_plan(tokens, routes, probs, up_weight, down_weight, old_place, new_place):
+    n = lax.axis_size("expert")
+    rows = tokens.shape[1]
+    dense = (
+        routes.shape[2] == old_place.shape[0] == n
+        and n % 2 == 0
+        and lax.axis_size("tensor") == tokens.shape[0] == 2
+        and up_weight.shape[0] == 1
+        and rows % 32 == 0
+        and up_weight.shape[2] % 128 == 0
+    )
+    plan = dense_on_device if dense else on_device
+    return plan(tokens, routes, probs, up_weight, down_weight, old_place, new_place)
+
+
 def solution(mesh):
     placed = (
         P(None, ("groups", "expert"), None),
@@ -114,7 +363,7 @@
         P("groups"),
     )
     return jax.shard_map(
-        on_device,
+        choose_plan,
         mesh=mesh,
         in_specs=placed,
         out_specs=(P(None, ("groups", "expert"), "tensor"), P(("groups", "expert"))),

time: 183 us -> 91.7 us (0.50)
  waiting for transfers between devices: 104 us -> 0 us
  Pallas kernels: 0 us -> 82.6 us
  blocking collectives: 30.5 us -> 0 us
  starting transfers between devices: 19.6 us -> 0 us
  matrix products: 19.2 us -> 0 us
  local copies, waits for them, and re-layouts: 2.12 us -> 5.16 us
  other arithmetic: 5.9 us -> 2.98 us
    all_to_all x4 -> x0, waiting for transfers between devices: 104 us -> none  [the longest x2 85.9 us: serve_cells(): lax.all_to_all(send_rows, 'expert', split_axis=0, concat_axis=0, tiled=True)]
    pallas_call x0 -> x1, Pallas kernels: none -> 82.6 us  [dense_on_device(): pl.pallas_call(functools.partial(expert_kernel, n, chunks), out_shape=jax...]
    psum x1 -> x0, blocking collectives: 25.8 us -> none  [on_device(): slot_counts = lax.psum(jnp.sum(chosen.astype(jnp.int32), axis=0), 'expert')]
    all_to_all x4 -> x0, starting transfers between devices: 19.6 us -> none  [the longest x2 11.7 us: serve_cells(): lax.all_to_all(send_rows, 'expert', split_axis=0, concat_axis=0, tiled=True)]
    dot_general x8 -> x0, matrix products: 19.2 us -> none  [the longest x2 6.73 us: serve_cells(): jnp.einsum('nscd,sdf->nscf', grid, up_local, preferred_element_type=jnp.f...]
    all_gather x2 -> x0, blocking collectives: 4.74 us -> none  [serve_cells(): hidden = lax.all_gather(hidden, 'tensor', axis=3, tiled=True)]
    unnamed x6 -> x9, local copies, waits for them, and re-layouts: 0.02 us -> 4.56 us
    reduce_sum x10 -> x4, other arithmetic: 5.03 us -> 2.86 us  [the longest x1 1.02 us: dense_slot_rows(): counts = jnp.sum(hits.astype(jnp.int32), axis=(1, 2))]
  transfers between devices with their start and end apart: 4 -> 0, of which waited for: 3 -> 0; matrix products, arithmetic and copies ran while one was open for 8% -> 0% of each run, Pallas kernels for 0% -> 0%
where the time goes in v1:
time: 91.7 us; the launch traced here: 91.4 us
  Pallas kernels  82.6 us (90%)
  local copies, waits for them, and re-layouts  5.16 us (6%)
  other arithmetic  2.98 us (3%)
    pallas_call x1, Pallas kernels, dense_on_device(): pl.pallas_call(functools.partial(expert_kernel, n, chunks), out_shape=jax...  82.6 us
    unnamed x9, local copies, waits for them, and re-layouts  4.56 us

profile of v1, /device:TPU:0, one launch (start us, length us, event | category | flops | bytes accessed | tf_op | source)
XLA Modules:
  0.0 91.4 jit_solution(17939163155296943436)
XLA Ops:
  0.6 0.8 select_reduce_fusion
  1.4 0.9 convert_reduce_fusion.2
  2.3 0.1 iota_compare_fusion.1
  2.4 0.0 copy-start
  2.4 1.4 %copy-done = bf16[1,2048,384]{2,1,0:T(8,128)(2,1)S(1)} copy-done((bf16[1,2048,384]{2,1,0:T(8,128)(2,1)S(1)}, bf16[1,2048,384]{2,1,0:T(8,128)(2,1)}, u32[]{:S(2)}) %copy-start) | copy-done | bytes 1572888
  3.8 0.0 copy-start.1
  3.8 1.4 %copy-done.1 = bf16[1,768,1024]{2,1,0:T(8,128)(2,1)S(1)} copy-done((bf16[1,768,1024]{2,1,0:T(8,128)(2,1)S(1)}, bf16[1,768,1024]{2,1,0:T(8,128)(2,1)}, u32[]{:S(2)}) %copy-start.1) | copy-done | bytes 1572888
  5.2 0.0 copy-start.2
  5.2 1.0 %copy-done.2 = bf16[2,64,2048]{2,1,0:T(8,128)(2,1)S(1)} copy-done((bf16[2,64,2048]{2,1,0:T(8,128)(2,1)S(1)}, bf16[2,64,2048]{2,1,0:T(8,128)(2,1)}, u32[]{:S(2)}) %copy-start.2) | copy-done | bytes 524312
  6.3 0.0 copy-start.3
  6.3 82.6 %shard_map.86 = bf16[2,64,1024]{2,1,0:T(8,128)(2,1)S(1)} custom-call(bf16[2,64,2048]{2,1,0:T(8,128)(2,1)S(1)} %copy-done.2, f32[2,8,64]{2,1,0:T(8,128)S(1)} %add_select_fusion.wts, bf16[1,2048,384]{2,1,0:T(8,128)(2,1)S(1)} %copy-done, bf16[1,768,1024]{2,1,0:T(8,128)(2,1)S(1)} %copy-done.1), custom_call_target="tpu_custom_call" | custom-call | tf_op jit(solution)/shard_map/pallas_call | solution.py:313
  88.8 0.0 copy-done.3
  88.8 0.2 fusion.3
  89.1 1.0 %convert_reduce_fusion = s32[16]{0:T(128)S(1)} fusion(s32[16]{0:T(128)S(1)} %get-tuple-element.3, s32[16]{0:T(128)S(1)} %compare_select_fusion, s32[64,8]{0,1:T(8,128)S(1)} %iota_add_fusion, pred[16]{0:T(512)(128)(4,1)S(1)} %broadcast_compare_fusion), kind=kLoop, calls=%fused_computation.5 | loop fusion | flops 81904 | bytes 2256 | tf_op jit(solution)/shard_map/reduce_sum | solution.py:137
  90.1 0.6 dynamic_slice.3
  90.7 0.7 copy.12
  (7 shorter events, 0.0 us)
Async XLA Ops:
  2.4 1.4 %copy-start = (bf16[1,2048,384]{2,1,0:T(8,128)(2,1)S(1)}, bf16[1,2048,384]{2,1,0:T(8,128)(2,1)}, u32[]{:S(2)}) copy-start(bf16[1,2048,384]{2,1,0:T(8,128)(2,1)} %up.1) | copy-start | bytes 4718596
  3.8 1.4 %copy-start.1 = (bf16[1,768,1024]{2,1,0:T(8,128)(2,1)S(1)}, bf16[1,768,1024]{2,1,0:T(8,128)(2,1)}, u32[]{:S(2)}) copy-start(bf16[1,768,1024]{2,1,0:T(8,128)(2,1)} %down.1) | copy-start | bytes 4718596
  5.2 1.0 %copy-start.2 = (bf16[2,64,2048]{2,1,0:T(8,128)(2,1)S(1)}, bf16[2,64,2048]{2,1,0:T(8,128)(2,1)}, u32[]{:S(2)}) copy-start(bf16[2,64,2048]{2,1,0:T(8,128)(2,1)} %tok.1) | copy-start | bytes 1572868
  6.3 82.6 %copy-start.3 = (s32[16]{0:T(128)S(1)}, s32[16]{0:T(128)}, u32[]{:S(2)}) copy-start(s32[16]{0:T(128)} %param.13) | copy-start | bytes 196

commit v2 on v1

--- a/solution.py
+++ b/solution.py
@@ -141,7 +141,7 @@
 def expert_kernel(
     n, chunks, tok, wts, up, down, out,
     xall, wall, upv, downv, acc, psend, xrecv, zsend, zrecv, res,
-    loc, tw_s, tw_r, w_s, w_r, az_s, az_r, ax_s, ax_r, rx_s, rx_r, rz_s, rz_r,
+    loc, tw_s, tw_r, w_s, w_r, own_s, az_s, az_r, ax_s, ax_r, rx_s, rx_r, rz_s, rz_r,
 ):
     e = lax.axis_index("expert")
     core = lax.axis_index("tensor")
@@ -162,11 +162,17 @@
             device_id=device, device_id_type=MESH,
         )
 
-    def column_id(step):
-        return lax.rem(z - step + column, column)
-
-    def block(step, side):
-        return 2 * column_id(step) + side
+    def place(p):
+        if p == 0:
+            return z, 0, 0
+        near = jnp.minimum(z, column - 1 - z)
+        both = p <= 2 * near
+        distance = jnp.where(both, (p + 1) // 2, p - near)
+        away = jnp.where(both, 1 - 2 * (p % 2), jnp.where(z > near, 1, -1))
+        return z - away * distance, distance, away
+
+    def block(p, side):
+        return 2 * place(p)[0] + side
 
     local = [
         pltpu.make_async_copy(tok.at[core], xall.at[e], loc.at[0]),
@@ -188,17 +194,24 @@
     def part(k):
         return pl.ds(k * step_rows, step_rows)
 
-    own_x, own_z, own_w = [], [], []
+    def inside(position):
+        return (position >= 0) & (position < column)
+
+    own_x, own_w, sent, guarded = [], [], [], []
+
+    def send_if(condition, copy):
+        pl.when(condition)(copy.start)
+        guarded.append((condition, copy))
+
     for k in range(chunks):
         copy = remote(tok.at[core, part(k)], xall.at[e, part(k)], ax_s.at[0, k], ax_r.at[0, k], pair)
         copy.start()
         own_x.append(copy)
-    for s in range(1, column):
-        for k in range(chunks):
-            target = 2 * lax.rem(z + s, column) + x
-            copy = remote(tok.at[core, part(k)], xall.at[e, part(k)], az_s.at[s, k], az_r.at[s, k], target)
-            copy.start()
-            own_z.append(copy)
+        for side in range(2):
+            target = z + 1 - 2 * side
+            send_if(inside(target), remote(
+                tok.at[core, part(k)], xall.at[e, part(k)], own_s.at[side, k], az_r.at[z, k], 2 * target + x
+            ))
     swap = [
         remote(
             up.at[0], upv.at[:, pl.ds(pl.multiple_of(core * up_half, 128), up_half)], tw_s.at[0], tw_r.at[0]
@@ -212,13 +225,15 @@
         copy.start()
         own_w.append(copy)
 
-    sent = []
-
-    def relay(s):
-        b = block(s, x)
+    def relay(p):
+        j, distance, away = place(p)
+        b = 2 * j + x
         for k in range(chunks):
-            remote(tok.at[core, part(k)], xall.at[b, part(k)], az_s.at[s, k], az_r.at[s, k], pair).wait_recv()
-            copy = remote(xall.at[b, part(k)], xall.at[b, part(k)], ax_s.at[s, k], ax_r.at[s, k], pair)
+            remote(tok.at[core, part(k)], xall.at[b, part(k)], az_s.at[p, k], az_r.at[j, k], pair).wait_recv()
+            send_if(inside(z + away), remote(
+                xall.at[b, part(k)], xall.at[b, part(k)], az_s.at[p, k], az_r.at[j, k], 2 * (z + away) + x
+            ))
+            copy = remote(xall.at[b, part(k)], xall.at[b, part(k)], ax_s.at[p, k], ax_r.at[p, k], pair)
             copy.start()
             sent.append(copy)
 
@@ -243,25 +258,44 @@
         for q in range(halves):
             acc[s, q] = jnp.dot(h, downv[q], preferred_element_type=jnp.float32) * scale
 
-    def give(s):
+    def offer(s):
         b = block(s, 1 - x)
         h = hidden_of(b)
         scale = scale_of(b)
         for q in range(halves):
             o = jnp.dot(h, downv[q], preferred_element_type=jnp.float32) * scale
             psend[s, q] = o.astype(jnp.bfloat16)
-            copy = remote(psend.at[s, q], xrecv.at[s, q], rx_s.at[s, q], rx_r.at[s, q], pair)
+            if s == column - 1:
+                give(s, q)
+
+    def give(s, q):
+        copy = remote(psend.at[s, q], xrecv.at[s, q], rx_s.at[s, q], rx_r.at[s, q], pair)
+        copy.start()
+        sent.append(copy)
+
+    def pass_on(p):
+        j, distance, away = place(p)
+        slot = jnp.where((distance == 1) & (away < 0), column, j)
+        outer = inside(z + away)
+        for q in range(halves):
+            remote(psend.at[p, q], xrecv.at[p, q], rx_s.at[p, q], rx_r.at[p, q], pair).wait_recv()
+
+            @pl.when(outer)
+            def _():
+                remote(zsend.at[p, q], zrecv.at[j, q], rz_s.at[p, q], rz_r.at[j, q], pair).wait_recv()
+                total = acc[p, q] + xrecv[p, q].astype(jnp.float32) + zrecv[j, q].astype(jnp.float32)
+                zsend[p, q] = total.astype(jnp.bfloat16)
+
+            @pl.when(jnp.logical_not(outer))
+            def _():
+                zsend[p, q] = (acc[p, q] + xrecv[p, q].astype(jnp.float32)).astype(jnp.bfloat16)
+
+            copy = remote(zsend.at[p, q], zrecv.at[slot, q], rz_s.at[p, q], rz_r.at[slot, q], 2 * (z - away) + x)
             copy.start()
             sent.append(copy)
 
-    def pass_on(s):
-        for q in range(halves):
-            remote(psend.at[s, q], xrecv.at[s, q], rx_s.at[s, q], rx_r.at[s, q], pair).wait_recv()
-            zsend[s, q] = (acc[s, q] + xrecv[s, q].astype(jnp.float32)).astype(jnp.bfloat16)
-            copy = remote(zsend.at[s, q], zrecv.at[s, q], rz_s.at[s, q], rz_r.at[s, q], block(s, x))
-            copy.start()
-            sent.append(copy)
-
+    if column > 1:
+        relay(1)
     for copy in local:
         copy.wait()
     for copy in swap:
@@ -269,32 +303,38 @@
     for s in range(1, n):
         remote(wts.at[core], wall.at[lax.rem(e - s + n, n)], w_s.at[s], w_r.at[s], pair).wait_recv()
     keep(0)
-    relay(1)
-    arrived(0)
-    give(0)
-    for s in range(1, column):
-        if s + 1 < column:
-            relay(s + 1)
-        keep(s)
-        arrived(s)
-        give(s)
-        if s > 1:
-            pass_on(s - 1)
-    if column > 1:
-        pass_on(column - 1)
+    for p in range(2, column):
+        relay(p)
+        keep(p - 1)
+    for p in range(column):
+        if p == column - 1 and p > 0:
+            keep(p)
+        arrived(p)
+        offer(p)
+    for p in range(column - 2, -1, -1):
+        for q in range(halves):
+            give(p, q)
+    for p in range(column - 1, 0, -1):
+        pass_on(p)
     for q in range(halves):
         remote(psend.at[0, q], xrecv.at[0, q], rx_s.at[0, q], rx_r.at[0, q], pair).wait_recv()
-        total = acc[0, q] + xrecv[0, q].astype(jnp.float32)
-        for s in range(1, column):
-            remote(zsend.at[s, q], zrecv.at[s, q], rz_s.at[s, q], rz_r.at[s, q], pair).wait_recv()
-            total = total + zrecv[s, q].astype(jnp.float32)
-        res[q] = total.astype(jnp.bfloat16)
+        acc[0, q] += xrecv[0, q].astype(jnp.float32)
+        for side, slot in ((1, z), (-1, column)):
+
+            @pl.when(inside(z + side))
+            def _():
+                remote(zsend.at[0, q], zrecv.at[slot, q], rz_s.at[0, q], rz_r.at[slot, q], pair).wait_recv()
+                acc[0, q] += zrecv[slot, q].astype(jnp.float32)
+
+        res[q] = acc[0, q].astype(jnp.bfloat16)
     last = remote(res.at[1 - core], out.at[core], tw_s.at[2], tw_r.at[2])
     last.start()
     mine = pltpu.make_async_copy(res.at[core], out.at[core], loc.at[4])
     mine.start()
-    for copy in own_x + own_z + own_w + swap + sent:
+    for copy in own_x + own_w + swap + sent:
         copy.wait_send()
+    for condition, copy in guarded:
+        pl.when(condition)(copy.wait_send)
     mine.wait()
     last.wait_send()
     remote(res.at[1 - core], out.at[1 - core], tw_s.at[2], tw_r.at[2]).wait_recv()
@@ -324,14 +364,14 @@
             pltpu.VMEM((column, 2, rows, half), bf16),
             pltpu.VMEM((column, 2, rows, half), bf16),
             pltpu.VMEM((column, 2, rows, half), bf16),
-            pltpu.VMEM((column, 2, rows, half), bf16),
+            pltpu.VMEM((column + 1, 2, rows, half), bf16),
             pltpu.VMEM((2, rows, half), bf16),
             dma((5,)), dma((3,)), dma((3,)), dma((n,)), dma((n,)),
-            dma((column, chunks)), dma((column, chunks)), dma((column, chunks)), dma((column, chunks)),
-            dma((column, 2)), dma((column, 2)), dma((column, 2)), dma((column, 2)),
+            dma((2, chunks)), dma((column, chunks)), dma((column, chunks)), dma((column, chunks)), dma((column, chunks)),
+            dma((column, 2)), dma((column, 2)), dma((column, 2)), dma((column + 1, 2)),
         ],
         compiler_params=pltpu.CompilerParams(
-            collective_id=0, has_side_effects=True, vmem_limit_bytes=40 * 1024 * 1024
+            collective_id=0, has_side_effects=True, vmem_limit_bytes=60 * 1024 * 1024
         ),
     )(tokens, weights, up_weight, down_weight)
     return (mixed, slot_rows)

time: 91.7 us -> 66 us (0.72)
  Pallas kernels: 82.6 us -> 58.8 us
  local copies, waits for them, and re-layouts: 5.16 us -> 2.27 us
    pallas_call x1, Pallas kernels: 82.6 us -> 58.8 us  [dense_on_device(): pl.pallas_call(functools.partial(expert_kernel, n, chunks), out_shape=jax...]
    unnamed x9 -> x3, local copies, waits for them, and re-layouts: 4.56 us -> 1.67 us
where the time goes in v2:
time: 66 us; the launch traced here: 65.4 us
  Pallas kernels  58.8 us (89%)
  other arithmetic  3.57 us (5%)
  local copies, waits for them, and re-layouts  2.27 us (3%)
  between operations  0.68 us (1%)
    pallas_call x1, Pallas kernels, dense_on_device(): pl.pallas_call(functools.partial(expert_kernel, n, chunks), out_shape=jax...  58.8 us
    unnamed x3, local copies, waits for them, and re-layouts  1.67 us

profile of v2, /device:TPU:0, one launch (start us, length us, event | category | flops | bytes accessed | tf_op | source)
XLA Modules:
  0.0 65.4 jit_solution(8576793462846662006)
XLA Ops:
  0.6 0.8 %select_reduce_fusion = f32[2,8,64]{2,1,0:T(8,128)S(1)} fusion(f32[2,64,8]{1,2,0:T(8,128)} %param.9, s32[2,64,8]{1,2,0:T(8,128)} %param.8, s32[8]{0:T(128)} %param.12), kind=kLoop, calls=%fused_computation.6 | loop fusion | flops 23552 | bytes 12320 | tf_op jit(solution)/shard_map/reduce_sum | solution.py:123
  1.4 0.9 %convert_reduce_fusion.2 = s32[8]{0:T(128)S(1)} fusion(s32[16]{0:T(128)} %param.13, s32[8]{0:T(128)} %param.12), kind=kLoop, calls=%fused_computation.16 | loop fusion | flops 376 | bytes 128 | tf_op jit(solution)/shard_map/reduce_sum | solution.py:117
  2.3 0.1 iota_compare_fusion.1
  2.4 0.6 add_select_fusion.wts
  3.0 0.0 copy-start
  3.0 58.8 %shard_map.86 = bf16[2,64,1024]{2,1,0:T(8,128)(2,1)} custom-call(bf16[2,64,2048]{2,1,0:T(8,128)(2,1)} %tok.1, f32[2,8,64]{2,1,0:T(8,128)} %add_select_fusion.wts, bf16[1,2048,384]{2,1,0:T(8,128)(2,1)} %up.1, bf16[1,768,1024]{2,1,0:T(8,128)(2,1)} %down.1), custom_call_target="tpu_custom_call" | custom-call | tf_op jit(solution)/shard_map/pallas_call | solution.py:353
  61.8 0.0 copy-done
  61.9 0.2 fusion.3
  62.1 1.0 %convert_reduce_fusion = s32[16]{0:T(128)S(1)} fusion(s32[16]{0:T(128)S(1)} %get-tuple-element.3, s32[16]{0:T(128)S(1)} %compare_select_fusion, s32[64,8]{0,1:T(8,128)S(1)} %iota_add_fusion, pred[16]{0:T(512)(128)(4,1)S(1)} %broadcast_compare_fusion), kind=kLoop, calls=%fused_computation.5 | loop fusion | flops 81904 | bytes 2256 | tf_op jit(solution)/shard_map/reduce_sum | solution.py:137
  63.1 0.6 dynamic_slice.3
  63.7 1.7 %copy.12 = bf16[2,64,1024]{2,1,0:T(8,128)(2,1)} copy(bf16[2,64,1024]{2,1,0:T(8,128)(2,1)} %shard_map.86) | data formatting | bytes 524288
  (6 shorter events, 0.0 us)
Async XLA Ops:
  3.0 58.8 %copy-start = (s32[16]{0:T(128)S(1)}, s32[16]{0:T(128)}, u32[]{:S(2)}) copy-start(s32[16]{0:T(128)} %param.13) | copy-start | bytes 196

commit v3 on v2

--- a/solution.py
+++ b/solution.py
@@ -114,28 +114,26 @@
     block_rows = token_count * routes.shape[2]
     early_cap = capacity_for(block_rows, old_place.shape[0], token_count)
     later_cap = capacity_for(block_rows, new_place.shape[0], token_count)
-    replicas = jnp.sum((old_place[:, None] == new_place[None, :]).astype(jnp.int32), axis=1)
-    rank = jnp.arange(token_count, dtype=jnp.int32)[None, :]
-    early_kept = jnp.broadcast_to(rank < early_cap, (old_place.shape[0], token_count))
-    later_kept = rank < later_cap * replicas[:, None]
-    kept = jnp.stack([early_kept, later_kept])
+    same_slot = old_place[:, None] == new_place[None, :]
+    replicas = jnp.sum(same_slot.astype(jnp.int32), axis=1, keepdims=True)
+    limit = jnp.where(jnp.arange(2, dtype=jnp.int32)[:, None, None] == 0, early_cap, later_cap * replicas[None])
+    kept = jnp.arange(token_count, dtype=jnp.int32)[None, None, :] < limit
     same = routes[:, None, :, :] == old_place[None, :, None, None]
-    weights = jnp.sum(jnp.where(same, probs[:, None, :, :], 0.0), axis=3)
-    return jnp.where(kept, weights, 0.0)
+    return jnp.sum(jnp.where(same & kept[..., None], probs[:, None, :, :], 0.0), axis=3)
 
 
 def dense_slot_rows(new_place, source_index, devices, token_count):
-    slot_count = new_place.shape[0]
-    slot_dev = slot_count // devices
-    positions = jnp.arange(slot_count, dtype=jnp.int32)
-    same = new_place[:, None] == new_place[None, :]
-    replicas = jnp.sum(same.astype(jnp.int32), axis=1)
-    earlier = positions[None, :] < positions[:, None]
-    occurrence = jnp.sum((same & earlier).astype(jnp.int32), axis=1)
-    places = jnp.arange(token_count, dtype=jnp.int32)[:, None] + jnp.arange(devices, dtype=jnp.int32)[None, :]
-    hits = (places[None] % replicas[:, None, None]) == occurrence[:, None, None]
-    counts = jnp.sum(hits.astype(jnp.int32), axis=(1, 2))
-    return lax.dynamic_slice_in_dim(counts, source_index * slot_dev, slot_dev, 0)
+    slot_dev = new_place.shape[0] // devices
+    mine = source_index * slot_dev + jnp.arange(slot_dev, dtype=jnp.int32)
+    positions = jnp.arange(new_place.shape[0], dtype=jnp.int32)
+    at_mine = mine[:, None] == positions[None, :]
+    held = jnp.sum(jnp.where(at_mine, new_place[None, :], 0), axis=1)
+    same = held[:, None] == new_place[None, :]
+    replicas = jnp.sum(same.astype(jnp.int32), axis=1)[:, None]
+    occurrence = jnp.sum((same & (positions[None, :] < mine[:, None])).astype(jnp.int32), axis=1)[:, None]
+    first = jnp.arange(devices, dtype=jnp.int32)[None, :] - occurrence + replicas - 1
+    counts = (first + token_count) // replicas - first // replicas
+    return jnp.sum(counts, axis=1)
 
 
 def expert_kernel(

time: 66 us -> 65.5 us (level)
    reduce_sum x4 -> x5, other arithmetic: 2.86 us -> 3.5 us  [the longest x1 1.42 us: dense_weights(): jnp.sum(jnp.where(same & kept[..., None], probs[:, None, :, :], 0.0), axi...]
where the time goes in v3:
time: 65.5 us; the launch traced here: 64.9 us
  Pallas kernels  58.8 us (90%)
  other arithmetic  3.67 us (6%)
  local copies, waits for them, and re-layouts  1.67 us (3%)
  between operations  0.67 us (1%)
    pallas_call x1, Pallas kernels, dense_on_device(): pl.pallas_call(functools.partial(expert_kernel, n, chunks), out_shape=jax...  58.8 us
    unnamed x3, local copies, waits for them, and re-layouts  1.67 us
    reduce_sum x1, other arithmetic, dense_weights(): jnp.sum(jnp.where(same & kept[..., None], probs[:, None, :, :], 0.0), axi...  1.42 us

profile of v3, /device:TPU:0, one launch (start us, length us, event | category | flops | bytes accessed | tf_op | source)
XLA Modules:
  0.0 64.9 jit_solution(7341098104766271186)
XLA Ops:
  0.6 0.9 %convert_reduce_fusion = s32[8]{0:T(128)S(1)} fusion(s32[16]{0:T(128)} %param.15, s32[8]{0:T(128)} %param.14), kind=kLoop, calls=%fused_computation.2 | loop fusion | flops 376 | bytes 128 | tf_op jit(solution)/shard_map/reduce_sum | solution.py:118
  1.5 0.1 broadcast_select_fusion
  1.6 0.1 iota_compare_fusion
  1.7 1.4 %select_reduce_fusion.wts = f32[2,8,64]{2,1,0:T(8,128)} fusion(f32[2,64,8]{1,2,0:T(8,128)} %param.11, s32[2,64,8]{1,2,0:T(8,128)} %param.10, s32[8]{0:T(128)} %param.14, pred[2,8,64]{2,1,0:T(8,128)(4,1)S(1)} %iota_compare_fusion), kind=kLoop, calls=%fused_computation | loop fusion | flops 31744 | bytes 13344 | tf_op jit(solution)/shard_map/reduce_sum | solution.py:122
  3.1 0.0 copy-start
  3.1 58.8 %shard_map.86 = bf16[2,64,1024]{2,1,0:T(8,128)(2,1)} custom-call(bf16[2,64,2048]{2,1,0:T(8,128)(2,1)} %tok.1, f32[2,8,64]{2,1,0:T(8,128)} %select_reduce_fusion.wts, bf16[1,2048,384]{2,1,0:T(8,128)(2,1)} %up.1, bf16[1,768,1024]{2,1,0:T(8,128)(2,1)} %down.1), custom_call_target="tpu_custom_call" | custom-call | tf_op jit(solution)/shard_map/pallas_call | solution.py:351
  61.9 0.0 copy-done
  61.9 0.2 fusion.1
  62.1 0.2 fusion.2
  62.4 0.8 %fusion.5 = s32[2]{0:T(128)} fusion(s32[2]{0:T(128)S(1)} %get-tuple-element.4, s32[2]{0:T(128)S(1)} %get-tuple-element.3, s32[2]{0:T(128)S(1)} %fusion.6), kind=kLoop, calls=%fused_computation.13 | loop fusion | flops 350 | bytes 32 | tf_op jit(solution)/shard_map/reduce_sum | solution.py:136
  63.2 1.7 %copy.12 = bf16[2,64,1024]{2,1,0:T(8,128)(2,1)} copy(bf16[2,64,1024]{2,1,0:T(8,128)(2,1)} %shard_map.86) | data formatting | bytes 524288
  (4 shorter events, 0.0 us)
Async XLA Ops:
  3.1 58.9 %copy-start = (s32[16]{0:T(128)S(1)}, s32[16]{0:T(128)}, u32[]{:S(2)}) copy-start(s32[16]{0:T(128)} %param.15) | copy-start | bytes 196
